TPU v7x, 32 devices: a whole 2x2x4 slice. The times are simulated.
32 devices in a mesh: wide: 8 (over y, x, core), rep: 4 (over z).
Axes of the slice: x: 2, y: 2, z: 4, core: 2. Of those that a mesh axis runs over, the one named last changes fastest.
Arguments:
- record: bfloat16 [32, 256, 8192], P(('wide', 'rep')), may hold values from -90 to 90
- valid: int32 [32, 8192], P(('wide', 'rep')), may hold values 0 or 1
- sources: int32 [3], replicated, may hold values from 0 to 127
Outputs:
- stacks: float32 [128, 192, 8192], P('rep', None, 'wide')
Inputs may be any that keep to these rules, and one draw needn't show every extreme that they name: `sources`: block b holds the channels 64 * b to 64 * b + 63.
All inputs are finite; a program needn't handle non-finite values. No bound on the sum of `valid` on one device may be relied on, other than what follows from the above.
Results may differ from a plain program's by a relative error of at most 0.0014.
Values may be sent and summed in bfloat16 or wider, within the bound.
A program may use at most 320 MiB of HBM per device.

v0:
```python
import functools
import math

import jax
import jax.numpy as jnp
import numpy as np
from jax import lax
from jax.experimental import pallas as pl
from jax.experimental.pallas import tpu as pltpu
from jax.sharding import PartitionSpec as P

SRC = 64
LAGS = 128
HALF_SMOOTH = 5
EPSILON = 1e-05
LEVEL_SHARE = 0.2

VMEM_LIMIT = 56 * 1024 * 1024
TILE_LAGS = 2


def forward_table(length, bins):
    phase = 2.0 * math.pi / length * np.mod(np.outer(np.arange(1, bins + 1), np.arange(length)), length)
    return jnp.asarray(np.concatenate([np.cos(phase), -np.sin(phase)], axis=0), jnp.bfloat16)


def hann_window(length):
    return jnp.asarray(0.5 - 0.5 * np.cos(2.0 * math.pi / length * np.arange(length)), jnp.float32)[:, None]


def band_matrix(bins):
    rows = np.arange(bins)
    near = (np.abs(rows[:, None] - rows[None, :]) <= HALF_SMOOTH).astype(np.float32)
    return jnp.asarray(near, jnp.bfloat16), jnp.asarray(1.0 / near.sum(axis=1, keepdims=True), jnp.float32)


def rotation_tables(length, bins, total_windows):
    shifts = np.arange(LAGS) - LAGS // 2
    phase = 2.0 * math.pi / length * np.mod(np.outer(shifts, np.arange(1, bins + 1)), length)
    scale = 1.0 / math.sqrt(total_windows * bins)
    cos, sin = np.cos(phase) * scale, np.sin(phase) * scale
    return jnp.asarray(np.stack([np.concatenate([cos, cos], 1), np.concatenate([sin, sin], 1)], 1), jnp.float32)


def whiten_kernel(record_ref, valid_ref, table_ref, taper_ref, band_ref, inverse_count_ref, out_ref):
    bins = band_ref.shape[0]
    samples = record_ref[...].astype(jnp.float32)
    centered = samples - jnp.mean(samples, axis=0, keepdims=True)
    tapered = (centered * taper_ref[...]).astype(jnp.bfloat16)
    spectrum = jnp.dot(table_ref[...], tapered, preferred_element_type=jnp.float32)
    real, imag = spectrum[:bins], spectrum[bins:]
    magnitude = jnp.sqrt(real * real + imag * imag)
    band = band_ref[...]
    smooth = jnp.zeros_like(magnitude)
    rest = magnitude
    for _ in range(3):
        piece = rest.astype(jnp.bfloat16)
        rest = rest - piece.astype(jnp.float32)
        smooth = smooth + jnp.dot(band, piece, preferred_element_type=jnp.float32)
    smooth = smooth * inverse_count_ref[...]
    level = jnp.mean(magnitude, axis=0, keepdims=True)
    gain = valid_ref[...].astype(jnp.float32) / (smooth + (LEVEL_SHARE * level + EPSILON))
    out_ref[:bins] = (real * gain).astype(jnp.bfloat16)
    out_ref[bins:] = (imag * gain).astype(jnp.bfloat16)


def whiten(record, valid, wide_count):
    length, channels = record.shape
    bins = length // 2
    shard = channels // wide_count
    tile = min(512, shard)
    per = shard // tile
    band, inverse_count = band_matrix(bins)
    fixed = lambda i: (0, 0)
    return pl.pallas_call(
        whiten_kernel,
        grid=(channels // tile,),
        in_specs=[
            pl.BlockSpec((length, tile), lambda i: (0, i)),
            pl.BlockSpec((1, tile), lambda i: (0, i)),
            pl.BlockSpec((2 * bins, length), fixed),
            pl.BlockSpec((length, 1), fixed),
            pl.BlockSpec((bins, bins), fixed),
            pl.BlockSpec((bins, 1), fixed),
        ],
        out_specs=pl.BlockSpec((None, 2 * bins, tile), lambda i: (i // per, 0, i % per)),
        out_shape=jax.ShapeDtypeStruct((wide_count, 2 * bins, shard), jnp.bfloat16),
        compiler_params=pltpu.CompilerParams(vmem_limit_bytes=VMEM_LIMIT),
        name="whiten",
    )(record, valid, forward_table(length, bins), hann_window(length), band, inverse_count)


def rotate_split(source_ref, rotation_ref, high_ref, low_ref):
    windows, rows, depth = source_ref.shape
    for window in range(windows):
        source = source_ref[window].astype(jnp.float32)
        real, imag = source[:, : depth // 2], source[:, depth // 2 :]
        turned = jnp.concatenate([imag, -real], axis=1)
        for lag in range(rotation_ref.shape[0]):
            value = source * rotation_ref[lag, 0:1] + turned * rotation_ref[lag, 1:2]
            high = value.astype(jnp.bfloat16)
            at = (slice(lag * rows, (lag + 1) * rows), slice(window * depth, (window + 1) * depth))
            high_ref[at] = high
            low_ref[at] = (value - high.astype(jnp.float32)).astype(jnp.bfloat16)


def stack_kernel(source_ref, rotation_ref, receiver_ref, *rest):
    out_ref, high_ref, low_ref = rest[-3:]
    before_ref = rest[0] if len(rest) == 4 else None
    rotate_split(source_ref, rotation_ref, high_ref, low_ref)
    lags, rows, channels = out_ref.shape
    tile = min(256, channels)

    @pl.loop(0, channels // tile)
    def _(number):
        columns = pl.ds(pl.multiple_of(number * tile, tile), tile)
        receiver = receiver_ref[:, columns]
        total = jnp.dot(high_ref[...], receiver, preferred_element_type=jnp.float32)
        total = total + jnp.dot(low_ref[...], receiver, preferred_element_type=jnp.float32)
        total = total.reshape(lags, rows, tile)
        if before_ref is not None:
            total = total + before_ref[:, :, columns]
        out_ref[:, :, columns] = total


def add_stacks(source, rotation, receiver, before):
    windows, rows, depth = source.shape
    channels = receiver.shape[2]
    lags = rotation.shape[0]
    receiver = receiver.reshape(windows * depth, channels)
    block = pl.BlockSpec((TILE_LAGS, rows, channels), lambda i: (i, 0, 0))
    operands = [source, rotation, receiver]
    in_specs = [
        pl.BlockSpec((windows, rows, depth), lambda i: (0, 0, 0)),
        pl.BlockSpec((TILE_LAGS, 2, depth), lambda i: (i, 0, 0)),
        pl.BlockSpec((windows * depth, channels), lambda i: (0, 0)),
    ]
    if before is not None:
        operands.append(before)
        in_specs.append(block)
    flops = 4 * lags * rows * windows * depth * channels
    return pl.pallas_call(
        stack_kernel,
        grid=(lags // TILE_LAGS,),
        in_specs=in_specs,
        out_specs=block,
        out_shape=jax.ShapeDtypeStruct((lags, rows, channels), jnp.float32),
        scratch_shapes=[pltpu.VMEM((TILE_LAGS * rows, windows * depth), jnp.bfloat16)] * 2,
        input_output_aliases={} if before is None else {3: 0},
        compiler_params=pltpu.CompilerParams(vmem_limit_bytes=VMEM_LIMIT),
        cost_estimate=pl.CostEstimate(flops=flops, bytes_accessed=lags * rows * channels * 8, transcendentals=0),
        name="add_stacks",
    )(*operands)


def on_device(record, valid, sources):
    wide_count = lax.axis_size("wide")
    rep_count = lax.axis_size("rep")
    rep = lax.axis_index("rep")
    _, length, channels = record.shape
    bins = length // 2
    shard = channels // wide_count
    total_windows = wide_count * rep_count
    lags = LAGS // rep_count
    whitened = whiten(record[0], valid, wide_count)
    per_shard = shard // SRC
    picked = []
    for number in range(sources.shape[0]):
        block = sources[number]
        start = (block // per_shard, 0, block % per_shard * SRC)
        picked.append(lax.dynamic_slice(whitened, start, (1, length, SRC))[0])
    own_source = jnp.concatenate(picked, axis=1).T
    source = lax.all_gather(own_source, "rep")
    source = lax.all_gather(source, "wide", axis=1)
    receiver = lax.all_to_all(whitened, "wide", split_axis=0, concat_axis=0, tiled=True)
    rotation = lax.dynamic_slice_in_dim(rotation_tables(length, bins, total_windows), rep * lags, lags, 0)
    ring = [(i, (i + 1) % rep_count) for i in range(rep_count)]
    stacks = None
    for step in range(rep_count):
        later = lax.ppermute(receiver, "rep", ring) if step < rep_count - 1 else None
        owner = lax.rem(rep + rep_count - step, rep_count)
        here = lax.dynamic_index_in_dim(source, owner, 0, keepdims=False)
        for first in range(0, wide_count, 8):
            part = slice(first, min(first + 8, wide_count))
            stacks = add_stacks(here[part], rotation, receiver[part], stacks)
        receiver = later
    return stacks


def solution(mesh):
    return jax.shard_map(
        on_device,
        mesh=mesh,
        in_specs=(P(("wide", "rep"), None, None), P(("wide", "rep"), None), P()),
        out_specs=P("rep", None, "wide"),
        check_vma=False,
    )
```

profile of v0, /device:TPU:0, one launch (start us, length us, event | category | flops | bytes accessed | tf_op | source)
XLA Modules:
  0.0 475.1 jit_solution(1231211589366653679)
XLA Ops:
  6.5 0.0 all-gather.4.cloned.1.call-start
  6.5 1.4 fusion
  15.7 15.7 %whiten.1 = bf16[8,256,1024]{2,1,0:T(8,128)(2,1)} custom-call(bf16[256,8192]{1,0:T(8,128)(2,1)} %bitcast.23, s32[1,8192]{1,0:T(1,128)} %valid_ref.1, bf16[256,256]{1,0:T(8,128)(2,1)} %constant.105.clone.table_ref, f32[256,1]{1,0:T(8,128)} %constant.110.taper_ref, bf16[128,128]{1,0:T(8,128)(2,1)} %constant.103.clone.band_ref, ...), custom_call_target="tpu_custom_call" | custom-call | tf_op jit(solution)/shard_map/whiten/pallas_call | solution.py:75
  31.4 1.0 constant_dynamic-slice_fusion.3
  32.4 0.1 copy.12
  32.5 0.1 copy.13
  32.6 0.1 copy.14
  32.7 16.8 %all-gather = bf16[768,256]{1,0:T(8,128)(2,1)} all-gather(bf16[192,256]{1,0:T(8,128)(2,1)S(1)} %maximum_bitcast_fusion), channel_id=2, replica_groups=mesh['wide'=8,'rep'=4] {'rep'}, dimensions={0}, use_global_device_ids=true | all-gather | bytes 491520 | tf_op jit(solution)/shard_map/all_gather | solution.py:173
  49.5 0.0 all-gather.4.cloned.1.call-update
  49.5 4.6 all-to-all-start
  54.1 1.5 constant_dynamic-slice_fusion.rotation_ref
  55.6 60.3 %all-to-all-done = bf16[8,256,1024]{2,1,0:T(8,128)(2,1)} async-done(((bf16[8,256,1024]{2,1,0:T(8,128)(2,1)}), bf16[8,256,1024]{2,1,0:T(8,128)(2,1)}, u32[]{:S(2)}, u32[]{:S(2)}) %all-to-all-start) | async-done | bytes 4194336 | tf_op jit(solution)/shard_map/all_to_all | solution.py:175
  115.8 2.3 collective-permute-start
  118.1 0.0 all-gather.4.cloned.1.call-done
  118.1 3.6 dynamic-slice_bitcast_fusion
  121.7 79.0 %add_stacks.4.rest_0_ = f32[32,192,1024]{2,1,0:T(8,128)} custom-call(bf16[8,192,256]{2,1,0:T(8,128)(2,1)} %get-tuple-element.8.source_ref, f32[32,2,256]{2,1,0:T(2,128)} %constant_dynamic-slice_fusion.rotation_ref, bf16[2048,1024]{1,0:T(8,128)(2,1)} %bitcast.17.receiver_ref), custom_call_target="tpu_custom_call" | custom-call | flops 51539607552 | bytes 50331648 | tf_op jit(solution)/shard_map/add_stacks/pallas_call | solution.py:142
  200.7 7.2 %collective-permute-done = bf16[8,256,1024]{2,1,0:T(8,128)(2,1)} collective-permute-done((bf16[8,256,1024]{2,1,0:T(8,128)(2,1)}, bf16[8,256,1024]{2,1,0:T(8,128)(2,1)}, u32[]{:S(2)}, u32[]{:S(2)}) %collective-permute-start) | collective-permute-done | bytes 4194336 | tf_op jit(solution)/shard_map/ppermute | solution.py:180
  207.9 0.2 collective-permute-start.1
  208.1 79.7 %add_stacks.5.rest_0_ = f32[32,192,1024]{2,1,0:T(8,128)} custom-call(bf16[8,192,256]{2,1,0:T(8,128)(2,1)} %get-tuple-element.9.source_ref, f32[32,2,256]{2,1,0:T(2,128)} %constant_dynamic-slice_fusion.rotation_ref, bf16[2048,1024]{1,0:T(8,128)(2,1)} %bitcast.15.receiver_ref, f32[32,192,1024]{2,1,0:T(8,128)} %add_stacks.4.rest_0_), custom_call_target="tpu_custom_call", output_to_operand_aliasing={{}: (3, {})} | custom-call | flops 51539607552 | bytes 50331648 | tf_op jit(solution)/shard_map/add_stacks/pallas_call | solution.py:142
  287.8 11.1 %collective-permute-done.1 = bf16[8,256,1024]{2,1,0:T(8,128)(2,1)S(1)} collective-permute-done((bf16[8,256,1024]{2,1,0:T(8,128)(2,1)}, bf16[8,256,1024]{2,1,0:T(8,128)(2,1)S(1)}, u32[]{:S(2)}, u32[]{:S(2)}) %collective-permute-start.1) | collective-permute-done | bytes 4194336 | tf_op jit(solution)/shard_map/ppermute | solution.py:180
  298.9 0.0 copy-start
  298.9 0.0 collective-permute-start.2
  298.9 2.0 copy-done
  300.8 79.7 %add_stacks.6.rest_0_ = f32[32,192,1024]{2,1,0:T(8,128)} custom-call(bf16[8,192,256]{2,1,0:T(8,128)(2,1)} %get-tuple-element.10.source_ref, f32[32,2,256]{2,1,0:T(2,128)} %constant_dynamic-slice_fusion.rotation_ref, bf16[2048,1024]{1,0:T(8,128)(2,1)} %bitcast.29, f32[32,192,1024]{2,1,0:T(8,128)} %add_stacks.5.rest_0_), custom_call_target="tpu_custom_call", output_to_operand_aliasing={{}: (3, {})} | custom-call | flops 51539607552 | bytes 50331648 | tf_op jit(solution)/shard_map/add_stacks/pallas_call | solution.py:142
  380.5 8.1 %collective-permute-done.2 = bf16[8,256,1024]{2,1,0:T(8,128)(2,1)} collective-permute-done((bf16[8,256,1024]{2,1,0:T(8,128)(2,1)S(1)}, bf16[8,256,1024]{2,1,0:T(8,128)(2,1)}, u32[]{:S(2)}, u32[]{:S(2)}) %collective-permute-start.2) | collective-permute-done | bytes 4194336 | tf_op jit(solution)/shard_map/ppermute | solution.py:180
  388.6 79.7 %add_stacks.7 = f32[32,192,1024]{2,1,0:T(8,128)} custom-call(bf16[8,192,256]{2,1,0:T(8,128)(2,1)} %get-tuple-element.11.source_ref, f32[32,2,256]{2,1,0:T(2,128)} %constant_dynamic-slice_fusion.rotation_ref, bf16[2048,1024]{1,0:T(8,128)(2,1)} %bitcast.11.receiver_ref, f32[32,192,1024]{2,1,0:T(8,128)} %add_stacks.6.rest_0_), custom_call_target="tpu_custom_call", output_to_operand_aliasing={{}: (3, {})} | custom-call | flops 51539607552 | bytes 50331648 | tf_op jit(solution)/shard_map/add_stacks/pallas_call | solution.py:142
  (1 shorter events, 0.0 us)
Async XLA Ops:
  6.5 111.6 %all-gather.4.cloned.1.call-start = ((), (), s32[]{:S(2)}) async-start(), calls=%async_computation.1 | async-start | bytes 3538944 | tf_op jit(solution)/shard_map/all_gather | solution.py:174
  49.5 66.3 %all-to-all-start = ((bf16[8,256,1024]{2,1,0:T(8,128)(2,1)}), bf16[8,256,1024]{2,1,0:T(8,128)(2,1)}, u32[]{:S(2)}, u32[]{:S(2)}) async-start(bf16[8,256,1024]{2,1,0:T(8,128)(2,1)} %whiten.1), calls=%async_computation | async-start | bytes 8388608 | tf_op jit(solution)/shard_map/all_to_all | solution.py:175
  115.8 92.1 %collective-permute-start = (bf16[8,256,1024]{2,1,0:T(8,128)(2,1)}, bf16[8,256,1024]{2,1,0:T(8,128)(2,1)}, u32[]{:S(2)}, u32[]{:S(2)}) collective-permute-start(bf16[8,256,1024]{2,1,0:T(8,128)(2,1)} %all-to-all-done), channel_id=1, source_target_pairs={{0,1},{1,2},{2,3},{3,0},{4,5},{5,6},{6,7},{7,4},{8,9},{9,10},{10,1... | collective-permute-start | bytes 12582920 | tf_op jit(solution)/shard_map/ppermute | solution.py:180
  207.9 90.9 %collective-permute-start.1 = (bf16[8,256,1024]{2,1,0:T(8,128)(2,1)}, bf16[8,256,1024]{2,1,0:T(8,128)(2,1)S(1)}, u32[]{:S(2)}, u32[]{:S(2)}) collective-permute-start(bf16[8,256,1024]{2,1,0:T(8,128)(2,1)} %collective-permute-done), channel_id=1, source_target_pairs={{0,1},{1,2},{2,3},{3,0},{4,5},{5,6},{6,7},{7,4},{8,9},{9,10},{10,1... | collective-permute-start | bytes 12582920 | tf_op jit(solution)/shard_map/ppermute | solution.py:180
  298.9 2.0 copy-start
  298.9 89.7 %collective-permute-start.2 = (bf16[8,256,1024]{2,1,0:T(8,128)(2,1)S(1)}, bf16[8,256,1024]{2,1,0:T(8,128)(2,1)}, u32[]{:S(2)}, u32[]{:S(2)}) collective-permute-start(bf16[8,256,1024]{2,1,0:T(8,128)(2,1)S(1)} %collective-permute-done.1), channel_id=1, source_target_pairs={{0,1},{1,2},{2,3},{3,0},{4,5},{5,6},{6,7},{7,4},{8,9},{9,10},{10,1... | collective-permute-start | bytes 12582920 | tf_op jit(solution)/shard_map/ppermute | solution.py:180
Sparse Core Ops, SparseCore 0:
  49.6 54.4 all-gather.3
where the time goes:
time: 483 us; the launch traced here: 475 us
  Pallas kernels  334 us (69%)
  waiting for transfers between devices  86.6 us (18%)
  between operations  21.2 us (4%)
  blocking collectives  16.8 us (3%)
  local copies, waits for them, and re-layouts  9.75 us (2%)
  starting transfers between devices  7.04 us (1%)
    pallas_call x4, Pallas kernels, add_stacks(): pl.pallas_call(stack_kernel, grid=(lags // TILE_LAGS,), in_specs=in_specs...  318 us
    all_to_all x1, waiting for transfers between devices, on_device(): lax.all_to_all(whitened, 'wide', split_axis=0, concat_axis=0, tiled=True)  60.3 us
    ppermute x3, waiting for transfers between devices, on_device(): lax.ppermute(receiver, 'rep', ring)  26.4 us
    all_gather x1, blocking collectives, on_device(): source = lax.all_gather(own_source, 'rep')  16.8 us
    pallas_call x1, Pallas kernels, whiten(): pl.pallas_call(whiten_kernel, grid=(channels // tile,), in_specs=[pl.Bloc...  15.7 us
  transfers between devices with their start and end apart: 5, of which 4 were waited for; matrix products, arithmetic and copies ran while one was open for 1% of the time, Pallas kernels for 50%

commit v1 on v0

v1 whole, which is shorter than its diff:
```python
import functools
import math

import jax
import jax.numpy as jnp
import numpy as np
from jax import lax
from jax.experimental import pallas as pl
from jax.experimental.pallas import tpu as pltpu
from jax.sharding import PartitionSpec as P

SRC = 64
LAGS = 128
HALF_SMOOTH = 5
EPSILON = 1e-05
LEVEL_SHARE = 0.2

VMEM_LIMIT = 56 * 1024 * 1024
TILE_LAGS = 4
LAST_TILE_LAGS = 2
PAIR = 2
RAISE = 2.0**16
MESH = pl.DeviceIdType.MESH


def forward_table(length, bins):
    phase = 2.0 * math.pi / length * np.mod(np.outer(np.arange(1, bins + 1), np.arange(length)), length)
    return jnp.asarray(np.concatenate([np.cos(phase), -np.sin(phase)], axis=0), jnp.bfloat16)


def hann_window(length):
    return jnp.asarray(0.5 - 0.5 * np.cos(2.0 * math.pi / length * np.arange(length)), jnp.float32)[:, None]


def band_matrix(bins):
    rows = np.arange(bins)
    near = (np.abs(rows[:, None] - rows[None, :]) <= HALF_SMOOTH).astype(np.float32)
    return jnp.asarray(near, jnp.bfloat16), jnp.asarray(1.0 / near.sum(axis=1, keepdims=True), jnp.float32)


def rotation_tables(length, bins):
    shifts = np.arange(LAGS) - LAGS // 2
    phase = 2.0 * math.pi / length * np.mod(np.outer(shifts, np.arange(1, bins + 1)), length)
    return jnp.asarray(np.stack([np.cos(phase), np.sin(phase)], 1) * RAISE, jnp.float32)


def whiten_tile(samples, flags, table, taper, band, inverse_count):
    bins = band.shape[0]
    samples = samples.astype(jnp.float32)
    centered = samples - jnp.mean(samples, axis=0, keepdims=True)
    tapered = (centered * taper).astype(jnp.bfloat16)
    spectrum = jnp.dot(table, tapered, preferred_element_type=jnp.float32)
    real, imag = spectrum[:bins], spectrum[bins:]
    magnitude = jnp.sqrt(real * real + imag * imag)
    smooth = jnp.zeros_like(magnitude)
    rest = magnitude
    for _ in range(3):
        piece = rest.astype(jnp.bfloat16)
        rest = rest - piece.astype(jnp.float32)
        smooth = smooth + jnp.dot(band, piece, preferred_element_type=jnp.float32)
    smooth = smooth * inverse_count
    level = jnp.mean(magnitude, axis=0, keepdims=True)
    gain = flags.astype(jnp.float32) / (smooth + (LEVEL_SHARE * level + EPSILON))
    return real * gain, imag * gain


def rotate_split(source, rotation_ref, first_lag, lags, high_ref, low_ref):
    for window in range(len(source)):
        spectrum = source[window].astype(jnp.float32)
        rows, depth = spectrum.shape
        half = depth // 2
        real, imag = spectrum[:, :half], spectrum[:, half:]
        for lag in range(lags):
            cos, sin = rotation_ref[first_lag + lag, 0:1], rotation_ref[first_lag + lag, 1:2]
            for part, value in enumerate((real * cos + imag * sin, imag * cos - real * sin)):
                high = value.astype(jnp.bfloat16)
                column = window * depth + part * half
                at = (slice(lag * rows, (lag + 1) * rows), slice(column, column + half))
                high_ref[at] = high
                low_ref[at] = (value - high.astype(jnp.float32)).astype(low_ref.dtype)


def gather_kernel(
    wide_count,
    rep_count,
    record_ref,
    valid_ref,
    picked_ref,
    picked_valid_ref,
    table_ref,
    taper_ref,
    band_ref,
    inverse_count_ref,
    rotation_ref,
    stacks_ref,
    last_receiver_ref,
    last_source_ref,
    spectra,
    sources,
    total,
    coarse,
    high_a,
    low_a,
    high_b,
    low_b,
    raw_sem,
    out_sem,
    send_sem,
    recv_sem,
    source_send_sem,
    source_recv_sem,
    share_sem,
):
    wide, rep = lax.axis_index("wide"), lax.axis_index("rep")
    slots = wide_count * rep_count
    forwarded = slots - wide_count
    length, shard = table_ref.shape[1], total.shape[1]
    rows = picked_ref.shape[1]
    bits = wide_count.bit_length() - 1
    following = (wide, lax.rem(rep + 1, rep_count))
    preceding = (wide, lax.rem(rep + rep_count - 1, rep_count))

    def peer(step):
        index = 0
        for bit in range(bits):
            index = index + ((wide // 2**bit + step // 2**bit) % 2) * 2**bit
        return index

    def slot_rows(slot):
        return pl.ds(pl.multiple_of(slot * length, length), length)

    def spectra_copy(source, target, device, sem):
        return pltpu.make_async_remote_copy(
            src_ref=spectra.at[slot_rows(source)],
            dst_ref=spectra.at[slot_rows(target)],
            send_sem=send_sem.at[sem],
            recv_sem=recv_sem.at[target],
            device_id=device,
            device_id_type=MESH,
        )

    def onward(slot):
        return spectra_copy(slot, slot + wide_count, following, slot)

    def exchange(step):
        return spectra_copy(slots - 1 + step, step, (peer(step), rep), forwarded + step)

    def source_copy(source, target, device, sem):
        return pltpu.make_async_remote_copy(
            src_ref=sources.at[source],
            dst_ref=sources.at[target],
            send_sem=sem,
            recv_sem=source_recv_sem.at[target],
            device_id=device,
            device_id_type=MESH,
        )

    def source_onward(step):
        return source_copy(step * wide_count, (step + 1) * wide_count, following, source_send_sem.at[step])

    def source_share(step, number):
        slot = step * wide_count
        return source_copy(slot, slot + number, (peer(number), rep), share_sem.at[slot + number])

    def raw_copy(step, slot):
        columns = pl.ds(pl.multiple_of(peer(step) * shard, shard), shard)
        return pltpu.make_async_copy(record_ref.at[:, columns], spectra.at[slot_rows(slot)], raw_sem.at[step])

    def wait_slot(slot):
        spectra_copy(slot, slot, following, slot).wait_recv()

    def wait_source(slot):
        source_copy(slot, slot, following, share_sem.at[slot]).wait_recv()

    def ready(slot):
        wait_slot(slot)

        @pl.when(slot < forwarded)
        def _():
            onward(slot).start()

    def share_sources(step):
        if step:
            wait_source(step * wide_count)
        if step < rep_count - 1:
            source_onward(step).start()

        @pl.loop(1, wide_count)
        def _(number):
            source_share(step, number).start()

    def whiten(step, slot):
        tile = min(512, shard)
        bins = length // 2

        @pl.loop(0, shard // tile)
        def _(number):
            columns = pl.ds(pl.multiple_of(number * tile, tile), tile)
            start = pl.multiple_of(peer(step) * shard + number * tile, tile)
            real, imag = whiten_tile(
                spectra[slot_rows(slot), columns],
                valid_ref[:, pl.ds(start, tile)],
                table_ref[...],
                taper_ref[...],
                band_ref[...],
                inverse_count_ref[...],
            )
            at = pl.multiple_of(slot * length, length)
            spectra[pl.ds(at, bins), columns] = real.astype(jnp.bfloat16)
            spectra[pl.ds(at + bins, bins), columns] = imag.astype(jnp.bfloat16)

    barrier = pltpu.get_barrier_semaphore()
    pl.semaphore_signal(barrier, inc=1, device_id=preceding, device_id_type=MESH)

    @pl.loop(1, wide_count)
    def _(step):
        pl.semaphore_signal(barrier, inc=1, device_id=(peer(step), rep), device_id_type=MESH)

    raw_copy(0, 0).start()

    @pl.loop(1, wide_count)
    def _(step):
        raw_copy(step, slots - 1 + step).start()

    real, imag = whiten_tile(
        picked_ref[...],
        picked_valid_ref[...],
        table_ref[...],
        taper_ref[...],
        band_ref[...],
        inverse_count_ref[...],
    )
    sources[0] = jnp.concatenate([real, imag], axis=0).T.astype(jnp.bfloat16)
    pl.semaphore_wait(barrier, wide_count)
    share_sources(0)
    raw_copy(0, 0).wait()
    whiten(0, 0)
    onward(0).start()

    @pl.loop(1, wide_count)
    def _(step):
        raw_copy(step, slots - 1 + step).wait()
        whiten(step, slots - 1 + step)
        exchange(step).start()

        @pl.when(step == 3)
        def _():
            ready(1)
            share_sources(1)

    total[...] = jnp.zeros_like(total)

    lags = LAGS // rep_count
    tiles = lags // TILE_LAGS
    tile_rows = TILE_LAGS * rows
    tile = min(256, shard)

    def add(pair, number, high_ref, low_ref):
        at = pl.ds(pl.multiple_of(number * tile_rows, tile_rows), tile_rows)
        depth = pl.ds(pl.multiple_of(pair * PAIR * length, PAIR * length), PAIR * length)
        for first in range(0, shard, tile):
            columns = slice(first, first + tile)
            value = jnp.dot(high_ref[...], spectra[depth, columns], preferred_element_type=jnp.float32)
            value = value + jnp.dot(low_ref[...], coarse[:, columns], preferred_element_type=jnp.float32)
            total[at, columns] += value

    @pl.loop(0, slots // PAIR - 1)
    def _(pair):
        first = pair * PAIR

        @pl.when(first < wide_count - PAIR)
        def _():
            ready(first + 2)

        @pl.when(first >= wide_count)
        def _():
            ready(first)
            ready(first + 1)

        @pl.when(first % wide_count != 0)
        def _():
            wait_source(first)

        wait_source(first + 1)
        for step in range(2, rep_count):

            @pl.when(pair == step - 2)
            def _():
                share_sources(step)

        coarse[...] = spectra[pl.ds(pl.multiple_of(first * length, PAIR * length), PAIR * length), :].astype(coarse.dtype)
        source = [sources.at[first + number] for number in range(PAIR)]

        def rotate(number, high_ref, low_ref):
            rotate_split([ref[...] for ref in source], rotation_ref, rep * lags + number * TILE_LAGS, TILE_LAGS, high_ref, low_ref)

        rotate(0, high_a, low_a)

        @pl.loop(0, tiles // 2)
        def _(double):
            number = double * 2
            add(pair, number, high_a, low_a)
            rotate(number + 1, high_b, low_b)
            add(pair, number + 1, high_b, low_b)
            rotate((number + 2) % tiles, high_a, low_a)

        @pl.when(first < wide_count - PAIR)
        def _():
            ready(first + 3)

    out = pltpu.make_async_copy(total, stacks_ref, out_sem.at[0])
    out.start()
    for slot in range(slots - PAIR, slots):
        wait_slot(slot)
        wait_source(slot)
    last = [
        pltpu.make_async_copy(spectra.at[pl.ds((slots - PAIR) * length, PAIR * length)], last_receiver_ref, out_sem.at[1]),
        pltpu.make_async_copy(sources.at[pl.ds(slots - PAIR, PAIR)], last_source_ref, out_sem.at[2]),
    ]
    for copy in last:
        copy.start()

    @pl.loop(0, forwarded)
    def _(slot):
        onward(slot).wait_send()

    @pl.loop(1, wide_count)
    def _(step):
        exchange(step).wait_send()

    for step in range(rep_count):
        if step < rep_count - 1:
            source_onward(step).wait_send()

        @pl.loop(1, wide_count)
        def _(number):
            source_share(step, number).wait_send()

    for copy in last:
        copy.wait()
    out.wait()


def gather_stacks(record, valid, picked, picked_valid, wide_count, rep_count):
    length, channels = record.shape
    bins = length // 2
    shard = channels // wide_count
    slots = wide_count * rep_count
    rows = picked.shape[1]
    lags = LAGS // rep_count
    band, inverse_count = band_matrix(bins)
    rotation = rotation_tables(length, bins)
    in_vmem = pl.BlockSpec(memory_space=pltpu.VMEM)
    anywhere = pl.BlockSpec(memory_space=pl.ANY)
    flops = 4 * lags * rows * slots * length * shard
    half = [pltpu.VMEM((TILE_LAGS * rows, PAIR * length), jnp.bfloat16), pltpu.VMEM((TILE_LAGS * rows, PAIR * length), jnp.float8_e5m2)]
    return pl.pallas_call(
        functools.partial(gather_kernel, wide_count, rep_count),
        in_specs=[anywhere] + [in_vmem] * 8,
        out_specs=[anywhere] * 3,
        out_shape=[
            jax.ShapeDtypeStruct((lags * rows, shard), jnp.float32),
            jax.ShapeDtypeStruct((PAIR * length, shard), jnp.bfloat16),
            jax.ShapeDtypeStruct((PAIR, rows, length), jnp.bfloat16),
        ],
        scratch_shapes=[
            pltpu.VMEM(((slots + wide_count - 1) * length, shard), jnp.bfloat16),
            pltpu.VMEM((slots, rows, length), jnp.bfloat16),
            pltpu.VMEM((lags * rows, shard), jnp.float32),
            pltpu.VMEM((PAIR * length, shard), jnp.float8_e5m2),
            *half,
            *half,
            pltpu.SemaphoreType.DMA((wide_count,)),
            pltpu.SemaphoreType.DMA((3,)),
            pltpu.SemaphoreType.DMA((slots,)),
            pltpu.SemaphoreType.DMA((slots,)),
            pltpu.SemaphoreType.DMA((rep_count,)),
            pltpu.SemaphoreType.DMA((slots,)),
            pltpu.SemaphoreType.DMA((slots,)),
        ],
        compiler_params=pltpu.CompilerParams(collective_id=0, has_side_effects=True, vmem_limit_bytes=VMEM_LIMIT),
        cost_estimate=pl.CostEstimate(flops=flops, bytes_accessed=lags * rows * shard * 4, transcendentals=0),
        name="gather_stacks",
    )(record, valid, picked, picked_valid, forward_table(length, bins), hann_window(length), band, inverse_count, rotation)


def last_kernel(scale, source_ref, rotation_ref, receiver_ref, before_ref, out_ref, high_ref, low_ref, coarse_ref):
    lags, rows, channels = out_ref.shape
    first_lag = (lax.axis_index("rep") * pl.num_programs(0) + pl.program_id(0)) * lags

    @pl.when(pl.program_id(0) == 0)
    def _():
        coarse_ref[...] = receiver_ref[...].astype(coarse_ref.dtype)

    rotate_split([source_ref[window] for window in range(source_ref.shape[0])], rotation_ref, first_lag, lags, high_ref, low_ref)
    tile = min(256, channels)
    for first in range(0, channels, tile):
        columns = slice(first, first + tile)
        value = jnp.dot(high_ref[...], receiver_ref[:, columns], preferred_element_type=jnp.float32)
        value = value + jnp.dot(low_ref[...], coarse_ref[:, columns], preferred_element_type=jnp.float32)
        value = (value + before_ref[:, columns]) * scale
        out_ref[:, :, columns] = value.reshape(lags, rows, tile)


def last_stacks(source, receiver, before, scale, rep_count):
    windows, rows, depth = source.shape
    channels = receiver.shape[1]
    lags = LAGS // rep_count
    rotation = rotation_tables(depth, depth // 2)
    return pl.pallas_call(
        functools.partial(last_kernel, scale),
        grid=(lags // LAST_TILE_LAGS,),
        in_specs=[
            pl.BlockSpec((windows, rows, depth), lambda i: (0, 0, 0)),
            pl.BlockSpec(rotation.shape, lambda i: (0, 0, 0)),
            pl.BlockSpec((windows * depth, channels), lambda i: (0, 0)),
            pl.BlockSpec((LAST_TILE_LAGS * rows, channels), lambda i: (i, 0)),
        ],
        out_specs=pl.BlockSpec((LAST_TILE_LAGS, rows, channels), lambda i: (i, 0, 0)),
        out_shape=jax.ShapeDtypeStruct((lags, rows, channels), jnp.float32),
        scratch_shapes=[
            pltpu.VMEM((LAST_TILE_LAGS * rows, windows * depth), jnp.bfloat16),
            pltpu.VMEM((LAST_TILE_LAGS * rows, windows * depth), jnp.float8_e5m2),
            pltpu.VMEM((windows * depth, channels), jnp.float8_e5m2),
        ],
        compiler_params=pltpu.CompilerParams(vmem_limit_bytes=VMEM_LIMIT),
        name="last_stacks",
    )(source, rotation, receiver, before)


def on_device(record, valid, sources):
    wide_count = lax.axis_size("wide")
    rep_count = lax.axis_size("rep")
    length = record.shape[1]
    starts = [sources[number] * SRC for number in range(sources.shape[0])]
    picked = jnp.concatenate([lax.dynamic_slice_in_dim(record[0], start, SRC, 1) for start in starts], axis=1)
    picked_valid = jnp.concatenate([lax.dynamic_slice_in_dim(valid, start, SRC, 1) for start in starts], axis=1)
    before, receiver, source = gather_stacks(record[0], valid, picked, picked_valid, wide_count, rep_count)
    scale = 1.0 / math.sqrt(wide_count * rep_count * (length // 2)) / RAISE
    return last_stacks(source, receiver, before, scale, rep_count)


def solution(mesh):
    return jax.shard_map(
        on_device,
        mesh=mesh,
        in_specs=(P(("wide", "rep"), None, None), P(("wide", "rep"), None), P()),
        out_specs=P("rep", None, "wide"),
        check_vma=False,
    )
```

time: 483 us -> 322 us (0.67); the launches traced: 475 us -> 322 us
  waiting for transfers between devices: 86.6 us -> 0 us
  between operations: 21.2 us -> 1.91 us
  Pallas kernels: 334 us -> 316 us
  blocking collectives: 16.8 us -> 0 us
  starting transfers between devices: 7.04 us -> 0 us
  local copies, waits for them, and re-layouts: 9.75 us -> 3.17 us
    all_to_all x1 -> x0, waiting for transfers between devices: 60.3 us -> none  [on_device(): lax.all_to_all(whitened, 'wide', split_axis=0, concat_axis=0, tiled=True)]
    ppermute x3 -> x0, waiting for transfers between devices: 26.4 us -> none  [on_device(): lax.ppermute(receiver, 'rep', ring)]
    pallas_call x5 -> x2, Pallas kernels: 334 us -> 316 us  [the longest x1 288 us: gather_stacks(): pl.pallas_call(functools.partial(gather_kernel, wide_count, rep_count), i...]
    all_gather x1 -> x0, blocking collectives: 16.8 us -> none  [on_device(): source = lax.all_gather(own_source, 'rep')]
  transfers between devices with their start and end apart: 5 -> 0, of which waited for: 4 -> 0; matrix products, arithmetic and copies ran while one was open for 1% -> 0% of each run, Pallas kernels for 50% -> 0%
where the time goes in v1:
time: 322 us
  Pallas kernels  316 us (98%)
    pallas_call x1, Pallas kernels, gather_stacks(): pl.pallas_call(functools.partial(gather_kernel, wide_count, rep_count), i...  288 us
    pallas_call x1, Pallas kernels, last_stacks(): pl.pallas_call(functools.partial(last_kernel, scale), grid=(lags // LAST_...  27.1 us

profile of v1, /device:TPU:0, one launch (start us, length us, event | category | flops | bytes accessed | tf_op | source)
XLA Modules:
  0.0 322.0 jit_solution(17732102366889755153)
XLA Ops:
  0.0 1.4 fusion
  3.3 0.8 constant_dynamic-slice_fusion.2
  4.0 0.7 pad_add_fusion.picked_valid_ref
  4.7 1.0 dynamic-slice_bitcast_fusion.2
  5.7 0.8 pad_maximum_fusion.picked_ref
  6.5 288.5 %gather_stacks.1 = (f32[6144,1024]{1,0:T(8,128)}, bf16[512,1024]{1,0:T(8,128)(2,1)}, bf16[2,192,256]{2,1,0:T(8,128)(2,1)}) custom-call(bf16[256,8192]{1,0:T(8,128)(2,1)} %bitcast.10, s32[1,8192]{1,0:T(1,128)} %valid_ref.1, bf16[256,192]{1,0:T(8,128)(2,1)} %pad_maximum_fusion.picked_ref, s32[1,192]{1,0:T(1,128)} %pad_add_fusion.picked_valid_ref, ...), custom_call_target="tpu_custom_call" | custom-call | flops 206158430208 | bytes 25165824 | tf_op jit(solution)/shard_map/gather_stacks/pallas_call | solution.py:357
  295.0 27.1 %last_stacks.1 = f32[32,192,1024]{2,1,0:T(8,128)} custom-call(bf16[2,192,256]{2,1,0:T(8,128)(2,1)} %get-tuple-element.8.source_ref, f32[128,2,128]{2,1,0:T(2,128)} %constant.24.clone.rotation_ref, bf16[512,1024]{1,0:T(8,128)(2,1)} %get-tuple-element.9.receiver_ref, f32[6144,1024]{1,0:T(8,128)} %get-tuple-element.10.before_ref), custom_call_target="tpu_custom_call" | custom-call | tf_op jit(solution)/shard_map/last_stacks/pallas_call | solution.py:410

commit v2 on v1

v2 whole, which is shorter than its diff:
```python
import functools
import math

import jax
import jax.numpy as jnp
import numpy as np
from jax import lax
from jax.experimental import pallas as pl
from jax.experimental.pallas import tpu as pltpu
from jax.sharding import PartitionSpec as P

SRC = 64
LAGS = 128
HALF_SMOOTH = 5
EPSILON = 1e-05
LEVEL_SHARE = 0.2

VMEM_LIMIT = 56 * 1024 * 1024
TILE_LAGS = 4
PAIR = 2
RAISE = 2.0**16
MESH = pl.DeviceIdType.MESH


def forward_table(length, bins):
    phase = 2.0 * math.pi / length * np.mod(np.outer(np.arange(1, bins + 1), np.arange(length)), length)
    return jnp.asarray(np.concatenate([np.cos(phase), -np.sin(phase)], axis=0), jnp.bfloat16)


def hann_window(length):
    return jnp.asarray(0.5 - 0.5 * np.cos(2.0 * math.pi / length * np.arange(length)), jnp.float32)[:, None]


def band_matrix(bins):
    rows = np.arange(bins)
    near = (np.abs(rows[:, None] - rows[None, :]) <= HALF_SMOOTH).astype(np.float32)
    return jnp.asarray(near, jnp.bfloat16), jnp.asarray(1.0 / near.sum(axis=1, keepdims=True), jnp.float32)


def rotation_tables(length, bins):
    shifts = np.arange(LAGS) - LAGS // 2
    phase = 2.0 * math.pi / length * np.mod(np.outer(shifts, np.arange(1, bins + 1)), length)
    return jnp.asarray(np.stack([np.cos(phase), np.sin(phase)], 1) * RAISE, jnp.float32)


def whiten_tile(samples, flags, table, taper, band, inverse_count):
    bins = band.shape[0]
    samples = samples.astype(jnp.float32)
    centered = samples - jnp.mean(samples, axis=0, keepdims=True)
    tapered = (centered * taper).astype(jnp.bfloat16)
    spectrum = jnp.dot(table, tapered, preferred_element_type=jnp.float32)
    real, imag = spectrum[:bins], spectrum[bins:]
    magnitude = jnp.sqrt(real * real + imag * imag)
    smooth = jnp.zeros_like(magnitude)
    rest = magnitude
    for _ in range(3):
        piece = rest.astype(jnp.bfloat16)
        rest = rest - piece.astype(jnp.float32)
        smooth = smooth + jnp.dot(band, piece, preferred_element_type=jnp.float32)
    smooth = smooth * inverse_count
    level = jnp.mean(magnitude, axis=0, keepdims=True)
    gain = flags.astype(jnp.float32) / (smooth + (LEVEL_SHARE * level + EPSILON))
    return real * gain, imag * gain


def rotate_split(source, rotation_ref, first_lag, lags, high_ref, low_ref):
    for window in range(len(source)):
        spectrum = source[window].astype(jnp.float32)
        rows, depth = spectrum.shape
        half = depth // 2
        real, imag = spectrum[:, :half], spectrum[:, half:]
        for lag in range(lags):
            cos, sin = rotation_ref[first_lag + lag, 0:1], rotation_ref[first_lag + lag, 1:2]
            for part, value in enumerate((real * cos + imag * sin, imag * cos - real * sin)):
                high = value.astype(jnp.bfloat16)
                column = window * depth + part * half
                at = (slice(lag * rows, (lag + 1) * rows), slice(column, column + half))
                high_ref[at] = high
                low_ref[at] = (value - high.astype(jnp.float32)).astype(low_ref.dtype)


def pick_kernel(blocks_ref, *refs):
    count = blocks_ref.shape[0]
    table_ref, taper_ref, band_ref, inverse_count_ref, out_ref = refs[2 * count :]
    real, imag = whiten_tile(
        jnp.concatenate([ref[...].astype(jnp.float32) for ref in refs[:count]], axis=1),
        jnp.concatenate([ref[...].astype(jnp.float32) for ref in refs[count : 2 * count]], axis=1),
        table_ref[...],
        taper_ref[...],
        band_ref[...],
        inverse_count_ref[...],
    )
    turned = jnp.concatenate([real, imag], axis=0).T
    for number in range(count):
        both = turned[number * 2 * SRC : (number + 1) * 2 * SRC]
        chosen = jnp.where(blocks_ref[number] % 2 == 1, both[SRC:], both[:SRC])
        out_ref[number * SRC : (number + 1) * SRC] = chosen.astype(jnp.bfloat16)


def pick_sources(record, valid, blocks):
    length = record.shape[0]
    bins = length // 2
    count = blocks.shape[0]
    band, inverse_count = band_matrix(bins)

    def block_specs(rows):
        return [pl.BlockSpec((rows, 2 * SRC), lambda i, at, number=number: (0, at[number] // 2)) for number in range(count)]

    in_vmem = pl.BlockSpec(memory_space=pltpu.VMEM)
    return pl.pallas_call(
        pick_kernel,
        grid_spec=pltpu.PrefetchScalarGridSpec(
            num_scalar_prefetch=1,
            grid=(1,),
            in_specs=block_specs(length) + block_specs(1) + [in_vmem] * 4,
            out_specs=pl.BlockSpec((count * SRC, length), lambda i, at: (0, 0)),
        ),
        out_shape=jax.ShapeDtypeStruct((count * SRC, length), jnp.bfloat16),
        name="pick_sources",
    )(blocks, *[record] * count, *[valid] * count, forward_table(length, bins), hann_window(length), band, inverse_count)


def gather_kernel(
    wide_count,
    rep_count,
    record_ref,
    valid_ref,
    picked_ref,
    table_ref,
    taper_ref,
    band_ref,
    inverse_count_ref,
    rotation_ref,
    total,
    last_receiver_ref,
    last_source_ref,
    raw,
    spectra,
    sources,
    coarse,
    high_a,
    low_a,
    high_b,
    low_b,
    raw_sem,
    send_sem,
    recv_sem,
    source_send_sem,
    source_recv_sem,
    share_sem,
):
    wide, rep = lax.axis_index("wide"), lax.axis_index("rep")
    slots = wide_count * rep_count
    forwarded = slots - wide_count
    length, shard = table_ref.shape[1], total.shape[1]
    rows = sources.shape[1]
    bits = wide_count.bit_length() - 1
    following = (wide, lax.rem(rep + 1, rep_count))
    preceding = (wide, lax.rem(rep + rep_count - 1, rep_count))

    def peer(step):
        index = 0
        for bit in range(bits):
            index = index + ((wide // 2**bit + step // 2**bit) % 2) * 2**bit
        return index

    def slot_rows(slot):
        return pl.ds(pl.multiple_of(slot * length, length), length)

    def shard_columns(step):
        return pl.ds(pl.multiple_of(peer(step) * shard, shard), shard)

    def spectra_copy(source, target, device, sem):
        return pltpu.make_async_remote_copy(
            src_ref=spectra.at[slot_rows(source)],
            dst_ref=spectra.at[slot_rows(target)],
            send_sem=send_sem.at[sem],
            recv_sem=recv_sem.at[target],
            device_id=device,
            device_id_type=MESH,
        )

    def onward(slot):
        return spectra_copy(slot, slot + wide_count, following, slot)

    def exchange(step):
        return pltpu.make_async_remote_copy(
            src_ref=raw.at[:, shard_columns(step)],
            dst_ref=spectra.at[slot_rows(step)],
            send_sem=send_sem.at[forwarded + step],
            recv_sem=recv_sem.at[step],
            device_id=(peer(step), rep),
            device_id_type=MESH,
        )

    def source_copy(source, target, device, sem):
        return pltpu.make_async_remote_copy(
            src_ref=sources.at[source],
            dst_ref=sources.at[target],
            send_sem=sem,
            recv_sem=source_recv_sem.at[target],
            device_id=device,
            device_id_type=MESH,
        )

    def source_onward(step):
        return source_copy(step * wide_count, (step + 1) * wide_count, following, source_send_sem.at[step])

    def source_share(step, number):
        slot = step * wide_count
        return source_copy(slot, slot + number, (peer(number), rep), share_sem.at[slot + number])

    def wait_slot(slot):
        spectra_copy(slot, slot, following, slot).wait_recv()

    def wait_source(slot):
        source_copy(slot, slot, following, share_sem.at[slot]).wait_recv()

    def ready(slot):
        wait_slot(slot)

        @pl.when(slot < forwarded)
        def _():
            onward(slot).start()

    def share_sources(step):
        if step:
            wait_source(step * wide_count)
        if step < rep_count - 1:
            source_onward(step).start()

        @pl.loop(1, wide_count)
        def _(number):
            source_share(step, number).start()

    def whiten(step, out_ref, out_column):
        tile = min(512, shard)
        bins = length // 2

        @pl.loop(0, shard // tile)
        def _(number):
            start = pl.multiple_of(peer(step) * shard + number * tile, tile)
            real, imag = whiten_tile(
                raw[:, pl.ds(start, tile)],
                valid_ref[:, pl.ds(start, tile)],
                table_ref[...],
                taper_ref[...],
                band_ref[...],
                inverse_count_ref[...],
            )
            columns = pl.ds(pl.multiple_of(out_column + number * tile, tile), tile)
            out_ref[:bins, columns] = real.astype(jnp.bfloat16)
            out_ref[bins : 2 * bins, columns] = imag.astype(jnp.bfloat16)

    record = pltpu.make_async_copy(record_ref, raw, raw_sem)
    record.start()
    barrier = pltpu.get_barrier_semaphore()
    pl.semaphore_signal(barrier, inc=1, device_id=preceding, device_id_type=MESH)

    @pl.loop(1, wide_count)
    def _(step):
        pl.semaphore_signal(barrier, inc=1, device_id=(peer(step), rep), device_id_type=MESH)

    sources[0] = picked_ref[...]
    pl.semaphore_wait(barrier, wide_count)
    share_sources(0)
    record.wait()
    whiten(0, spectra, 0)
    onward(0).start()

    @pl.loop(1, wide_count)
    def _(step):
        whiten(step, raw, peer(step) * shard)
        exchange(step).start()

        @pl.when(step == 3)
        def _():
            ready(1)
            share_sources(1)

    total[...] = jnp.zeros_like(total)

    lags = LAGS // rep_count
    tiles = lags // TILE_LAGS
    tile_rows = TILE_LAGS * rows
    tile = min(256, shard)

    def add(first, count, number, high_ref, low_ref):
        at = pl.ds(pl.multiple_of(number * tile_rows, tile_rows), tile_rows)
        depth = pl.ds(pl.multiple_of(first * length, length), count * length)
        for start in range(0, shard, tile):
            columns = slice(start, start + tile)
            value = jnp.dot(high_ref[:, : count * length], spectra[depth, columns], preferred_element_type=jnp.float32)
            low = low_ref[:, : count * length]
            value = value + jnp.dot(low, coarse[: count * length, columns], preferred_element_type=jnp.float32)
            total[at, columns] += value

    def add_windows(first, count):
        depth = pl.ds(pl.multiple_of(first * length, length), count * length)
        coarse[: count * length] = spectra[depth, :].astype(coarse.dtype)
        source = [sources.at[first + number] for number in range(count)]

        def rotate(number, high_ref, low_ref):
            rotate_split([ref[...] for ref in source], rotation_ref, rep * lags + number * TILE_LAGS, TILE_LAGS, high_ref, low_ref)

        rotate(0, high_a, low_a)

        @pl.loop(0, tiles // 2)
        def _(double):
            number = double * 2
            add(first, count, number, high_a, low_a)
            rotate(number + 1, high_b, low_b)
            add(first, count, number + 1, high_b, low_b)
            rotate((number + 2) % tiles, high_a, low_a)

    @pl.loop(0, slots // PAIR - 1)
    def _(pair):
        first = pair * PAIR

        @pl.when(first < wide_count - PAIR)
        def _():
            ready(first + 2)

        @pl.when(first >= wide_count)
        def _():
            ready(first)
            ready(first + 1)

        @pl.when(first % wide_count != 0)
        def _():
            wait_source(first)

        wait_source(first + 1)
        for step in range(2, rep_count):

            @pl.when(pair == step - 2)
            def _():
                share_sources(step)

        add_windows(first, PAIR)

        @pl.when(first < wide_count - PAIR)
        def _():
            ready(first + 3)

    wait_slot(slots - 2)
    wait_source(slots - 2)
    add_windows(slots - 2, 1)
    wait_slot(slots - 1)
    wait_source(slots - 1)
    last_receiver_ref[...] = spectra[(slots - 1) * length :]
    last_source_ref[...] = sources[slots - 1]

    @pl.loop(0, forwarded)
    def _(slot):
        onward(slot).wait_send()

    @pl.loop(1, wide_count)
    def _(step):
        exchange(step).wait_send()

    for step in range(rep_count):
        if step < rep_count - 1:
            source_onward(step).wait_send()

        @pl.loop(1, wide_count)
        def _(number):
            source_share(step, number).wait_send()


def gather_stacks(record, valid, picked, wide_count, rep_count):
    length, channels = record.shape
    bins = length // 2
    shard = channels // wide_count
    slots = wide_count * rep_count
    rows = picked.shape[0]
    lags = LAGS // rep_count
    band, inverse_count = band_matrix(bins)
    rotation = rotation_tables(length, bins)
    in_vmem = pl.BlockSpec(memory_space=pltpu.VMEM)
    flops = 4 * lags * rows * slots * length * shard
    half = [pltpu.VMEM((TILE_LAGS * rows, PAIR * length), jnp.bfloat16), pltpu.VMEM((TILE_LAGS * rows, PAIR * length), jnp.float8_e5m2)]
    return pl.pallas_call(
        functools.partial(gather_kernel, wide_count, rep_count),
        in_specs=[pl.BlockSpec(memory_space=pl.ANY)] + [in_vmem] * 7,
        out_specs=[in_vmem] * 3,
        out_shape=[
            pltpu.VMEM((lags * rows, shard), jnp.float32),
            jax.ShapeDtypeStruct((length, shard), jnp.bfloat16),
            jax.ShapeDtypeStruct((rows, length), jnp.bfloat16),
        ],
        scratch_shapes=[
            pltpu.VMEM((length, channels), jnp.bfloat16),
            pltpu.VMEM((slots * length, shard), jnp.bfloat16),
            pltpu.VMEM((slots, rows, length), jnp.bfloat16),
            pltpu.VMEM((PAIR * length, shard), jnp.float8_e5m2),
            *half,
            *half,
            pltpu.SemaphoreType.DMA,
            pltpu.SemaphoreType.DMA((slots,)),
            pltpu.SemaphoreType.DMA((slots,)),
            pltpu.SemaphoreType.DMA((rep_count,)),
            pltpu.SemaphoreType.DMA((slots,)),
            pltpu.SemaphoreType.DMA((slots,)),
        ],
        compiler_params=pltpu.CompilerParams(collective_id=0, has_side_effects=True, vmem_limit_bytes=VMEM_LIMIT - 4 * lags * rows * shard),
        cost_estimate=pl.CostEstimate(flops=flops, bytes_accessed=lags * rows * shard * 4, transcendentals=0),
        name="gather_stacks",
    )(record, valid, picked, forward_table(length, bins), hann_window(length), band, inverse_count, rotation)


def last_kernel(scale, source_ref, rotation_ref, receiver_ref, before_ref, out_ref, high_a, low_a, high_b, low_b, coarse, stage_a, stage_b, sem):
    lags, rows, channels = stage_a.shape
    tiles = out_ref.shape[0] // lags
    first_lag = lax.axis_index("rep") * out_ref.shape[0]
    tile = min(256, channels)
    coarse[...] = receiver_ref[...].astype(coarse.dtype)

    def rotate(number, high_ref, low_ref):
        rotate_split([source_ref[...]], rotation_ref, first_lag + number * lags, lags, high_ref, low_ref)

    def write(number, stage, at):
        return pltpu.make_async_copy(stage, out_ref.at[pl.ds(number * lags, lags)], sem.at[at])

    def finish(number, high_ref, low_ref, stage):
        at = pl.ds(pl.multiple_of(number * lags * rows, lags * rows), lags * rows)
        for start in range(0, channels, tile):
            columns = slice(start, start + tile)
            value = jnp.dot(high_ref[...], receiver_ref[:, columns], preferred_element_type=jnp.float32)
            value = value + jnp.dot(low_ref[...], coarse[:, columns], preferred_element_type=jnp.float32)
            value = (value + before_ref[at, columns]) * scale
            stage[:, :, columns] = value.reshape(lags, rows, tile)

    rotate(0, high_a, low_a)

    @pl.loop(0, tiles // 2)
    def _(double):
        number = double * 2

        @pl.when(double > 0)
        def _():
            write(number - 2, stage_a, 0).wait()

        finish(number, high_a, low_a, stage_a)
        write(number, stage_a, 0).start()
        rotate(number + 1, high_b, low_b)

        @pl.when(double > 0)
        def _():
            write(number - 1, stage_b, 1).wait()

        finish(number + 1, high_b, low_b, stage_b)
        write(number + 1, stage_b, 1).start()
        rotate((number + 2) % tiles, high_a, low_a)

    write(tiles - 2, stage_a, 0).wait()
    write(tiles - 1, stage_b, 1).wait()


def last_stacks(source, receiver, before, scale, rep_count):
    rows, length = source.shape
    channels = receiver.shape[1]
    in_vmem = pl.BlockSpec(memory_space=pltpu.VMEM)
    half = [pltpu.VMEM((TILE_LAGS * rows, length), jnp.bfloat16), pltpu.VMEM((TILE_LAGS * rows, length), jnp.float8_e5m2)]
    return pl.pallas_call(
        functools.partial(last_kernel, scale),
        in_specs=[in_vmem] * 4,
        out_specs=pl.BlockSpec(memory_space=pl.ANY),
        out_shape=jax.ShapeDtypeStruct((LAGS // rep_count, rows, channels), jnp.float32),
        scratch_shapes=[
            *half,
            *half,
            pltpu.VMEM((length, channels), jnp.float8_e5m2),
            pltpu.VMEM((TILE_LAGS, rows, channels), jnp.float32),
            pltpu.VMEM((TILE_LAGS, rows, channels), jnp.float32),
            pltpu.SemaphoreType.DMA((2,)),
        ],
        compiler_params=pltpu.CompilerParams(vmem_limit_bytes=VMEM_LIMIT - 4 * before.size),
        name="last_stacks",
    )(source, rotation_tables(length, length // 2), receiver, before)


def on_device(record, valid, sources):
    wide_count = lax.axis_size("wide")
    rep_count = lax.axis_size("rep")
    length = record.shape[1]
    picked = pick_sources(record[0], valid, sources)
    before, receiver, source = gather_stacks(record[0], valid, picked, wide_count, rep_count)
    scale = 1.0 / math.sqrt(wide_count * rep_count * (length // 2)) / RAISE
    before = pltpu.with_memory_space_constraint(before, pltpu.VMEM)
    return last_stacks(source, receiver, before, scale, rep_count)


def solution(mesh):
    return jax.shard_map(
        on_device,
        mesh=mesh,
        in_specs=(P(("wide", "rep"), None, None), P(("wide", "rep"), None), P()),
        out_specs=P("rep", None, "wide"),
        check_vma=False,
    )
```

time: 322 us -> 305 us (0.947)
  Pallas kernels: 316 us -> 304 us
    pallas_call x1 -> x2, Pallas kernels: 27.1 us -> 16 us  [the longest x1 12.9 us: last_stacks(): pl.pallas_call(functools.partial(last_kernel, scale), in_specs=[in_vmem]...]
where the time goes in v2:
time: 305 us; the launch traced here: 304 us
  Pallas kernels  304 us (100%)
    pallas_call x1, Pallas kernels, gather_stacks(): pl.pallas_call(functools.partial(gather_kernel, wide_count, rep_count), i...  288 us
    pallas_call x1, Pallas kernels, last_stacks(): pl.pallas_call(functools.partial(last_kernel, scale), in_specs=[in_vmem]...  12.9 us

profile of v2, /device:TPU:0, one launch (start us, length us, event | category | flops | bytes accessed | tf_op | source)
XLA Modules:
  0.0 304.4 jit_solution(10900132192939441064)
XLA Ops:
  0.0 3.1 %pick_sources.1.picked_ref = bf16[192,256]{1,0:T(8,128)(2,1)} custom-call(s32[3]{0:T(128)} %blocks_ref.1, bf16[256,8192]{1,0:T(8,128)(2,1)} %bitcast.1, bf16[256,8192]{1,0:T(8,128)(2,1)} %bitcast.2, bf16[256,8192]{1,0:T(8,128)(2,1)} %bitcast.3, s32[1,8192]{1,0:T(1,128)} %valid_ref.1, s32[1,8192]{1,0:T(1,128)} %valid_ref.1, s32[1,8192]{1,0:T(1,128)} %valid_ref.1, ...), custom_call_target="tpu_custom_call" | custom-call | tf_op jit(solution)/shard_map/pick_sources/pallas_call | solution.py:110
  3.1 288.4 %gather_stacks.1 = (f32[6144,1024]{1,0:T(8,128)S(1)}, bf16[256,1024]{1,0:T(8,128)(2,1)}, bf16[192,256]{1,0:T(8,128)(2,1)}) custom-call(bf16[256,8192]{1,0:T(8,128)(2,1)} %bitcast.4, s32[1,8192]{1,0:T(1,128)} %valid_ref.1, bf16[192,256]{1,0:T(8,128)(2,1)} %pick_sources.1.picked_ref, bf16[256,256]{1,0:T(8,128)(2,1)} %constant.12.clone.refs_6_.table_ref, ...), custom_call_target="tpu_custom_call" | custom-call | flops 206158430208 | bytes 25165824 | tf_op jit(solution)/shard_map/gather_stacks/pallas_call | solution.py:383
  291.5 12.9 %last_stacks.1 = f32[32,192,1024]{2,1,0:T(8,128)} custom-call(bf16[192,256]{1,0:T(8,128)(2,1)} %get-tuple-element.8.source_ref, f32[128,2,128]{2,1,0:T(2,128)} %constant.14.clone.rotation_ref, bf16[256,1024]{1,0:T(8,128)(2,1)} %get-tuple-element.9.receiver_ref, f32[6144,1024]{1,0:T(8,128)S(1)} %get-tuple-element.10.before_ref), custom_call_target="tpu_custom_call" | custom-call | tf_op jit(solution)/shard_map/last_stacks/pallas_call | solution.py:465

commit v3 on v2

--- a/solution.py
+++ b/solution.py
@@ -170,6 +170,10 @@
     def shard_columns(step):
         return pl.ds(pl.multiple_of(peer(step) * shard, shard), shard)
 
+    def raw_copy(step):
+        columns = shard_columns(step)
+        return pltpu.make_async_copy(record_ref.at[:, columns], raw.at[:, columns], raw_sem.at[step])
+
     def spectra_copy(source, target, device, sem):
         return pltpu.make_async_remote_copy(
             src_ref=spectra.at[slot_rows(source)],
@@ -252,8 +256,10 @@
             out_ref[:bins, columns] = real.astype(jnp.bfloat16)
             out_ref[bins : 2 * bins, columns] = imag.astype(jnp.bfloat16)
 
-    record = pltpu.make_async_copy(record_ref, raw, raw_sem)
-    record.start()
+    @pl.loop(0, wide_count)
+    def _(step):
+        raw_copy(step).start()
+
     barrier = pltpu.get_barrier_semaphore()
     pl.semaphore_signal(barrier, inc=1, device_id=preceding, device_id_type=MESH)
 
@@ -264,12 +270,13 @@
     sources[0] = picked_ref[...]
     pl.semaphore_wait(barrier, wide_count)
     share_sources(0)
-    record.wait()
+    raw_copy(0).wait()
     whiten(0, spectra, 0)
     onward(0).start()
 
     @pl.loop(1, wide_count)
     def _(step):
+        raw_copy(step).wait()
         whiten(step, raw, peer(step) * shard)
         exchange(step).start()
 
@@ -343,6 +350,22 @@
         def _():
             ready(first + 3)
 
+    @pl.loop(1, wide_count)
+    def _(step):
+        exchange(step).wait_send()
+
+    for step in range(rep_count):
+        if step < rep_count - 1:
+            source_onward(step).wait_send()
+
+        @pl.loop(1, wide_count)
+        def _(number):
+            source_share(step, number).wait_send()
+
+    @pl.loop(0, forwarded - 4)
+    def _(slot):
+        onward(slot).wait_send()
+
     wait_slot(slots - 2)
     wait_source(slots - 2)
     add_windows(slots - 2, 1)
@@ -351,21 +374,9 @@
     last_receiver_ref[...] = spectra[(slots - 1) * length :]
     last_source_ref[...] = sources[slots - 1]
 
-    @pl.loop(0, forwarded)
+    @pl.loop(forwarded - 4, forwarded)
     def _(slot):
         onward(slot).wait_send()
-
-    @pl.loop(1, wide_count)
-    def _(step):
-        exchange(step).wait_send()
-
-    for step in range(rep_count):
-        if step < rep_count - 1:
-            source_onward(step).wait_send()
-
-        @pl.loop(1, wide_count)
-        def _(number):
-            source_share(step, number).wait_send()
 
 
 def gather_stacks(record, valid, picked, wide_count, rep_count):
@@ -386,8 +397,8 @@
         out_specs=[in_vmem] * 3,
         out_shape=[
             pltpu.VMEM((lags * rows, shard), jnp.float32),
-            jax.ShapeDtypeStruct((length, shard), jnp.bfloat16),
-            jax.ShapeDtypeStruct((rows, length), jnp.bfloat16),
+            pltpu.VMEM((length, shard), jnp.bfloat16),
+            pltpu.VMEM((rows, length), jnp.bfloat16),
         ],
         scratch_shapes=[
             pltpu.VMEM((length, channels), jnp.bfloat16),
@@ -396,7 +407,7 @@
             pltpu.VMEM((PAIR * length, shard), jnp.float8_e5m2),
             *half,
             *half,
-            pltpu.SemaphoreType.DMA,
+            pltpu.SemaphoreType.DMA((wide_count,)),
             pltpu.SemaphoreType.DMA((slots,)),
             pltpu.SemaphoreType.DMA((slots,)),
             pltpu.SemaphoreType.DMA((rep_count,)),
@@ -419,10 +430,15 @@
     def rotate(number, high_ref, low_ref):
         rotate_split([source_ref[...]], rotation_ref, first_lag + number * lags, lags, high_ref, low_ref)
 
-    def write(number, stage, at):
-        return pltpu.make_async_copy(stage, out_ref.at[pl.ds(number * lags, lags)], sem.at[at])
-
-    def finish(number, high_ref, low_ref, stage):
+    def write(number, stage, at, part):
+        columns = pl.ds(part * tile, tile)
+        return pltpu.make_async_copy(stage.at[:, :, columns], out_ref.at[pl.ds(number * lags, lags), :, columns], sem.at[at, part])
+
+    def wait_write(number, stage, at):
+        for part in range(channels // tile):
+            write(number, stage, at, part).wait()
+
+    def finish(number, high_ref, low_ref, stage, side):
         at = pl.ds(pl.multiple_of(number * lags * rows, lags * rows), lags * rows)
         for start in range(0, channels, tile):
             columns = slice(start, start + tile)
@@ -430,6 +446,7 @@
             value = value + jnp.dot(low_ref[...], coarse[:, columns], preferred_element_type=jnp.float32)
             value = (value + before_ref[at, columns]) * scale
             stage[:, :, columns] = value.reshape(lags, rows, tile)
+            write(number, stage, side, start // tile).start()
 
     rotate(0, high_a, low_a)
 
@@ -439,22 +456,20 @@
 
         @pl.when(double > 0)
         def _():
-            write(number - 2, stage_a, 0).wait()
-
-        finish(number, high_a, low_a, stage_a)
-        write(number, stage_a, 0).start()
+            wait_write(number - 2, stage_a, 0)
+
+        finish(number, high_a, low_a, stage_a, 0)
         rotate(number + 1, high_b, low_b)
 
         @pl.when(double > 0)
         def _():
-            write(number - 1, stage_b, 1).wait()
-
-        finish(number + 1, high_b, low_b, stage_b)
-        write(number + 1, stage_b, 1).start()
+            wait_write(number - 1, stage_b, 1)
+
+        finish(number + 1, high_b, low_b, stage_b, 1)
         rotate((number + 2) % tiles, high_a, low_a)
 
-    write(tiles - 2, stage_a, 0).wait()
-    write(tiles - 1, stage_b, 1).wait()
+    wait_write(tiles - 2, stage_a, 0)
+    wait_write(tiles - 1, stage_b, 1)
 
 
 def last_stacks(source, receiver, before, scale, rep_count):
@@ -473,7 +488,7 @@
             pltpu.VMEM((length, channels), jnp.float8_e5m2),
             pltpu.VMEM((TILE_LAGS, rows, channels), jnp.float32),
             pltpu.VMEM((TILE_LAGS, rows, channels), jnp.float32),
-            pltpu.SemaphoreType.DMA((2,)),
+            pltpu.SemaphoreType.DMA((2, channels // min(256, channels))),
         ],
         compiler_params=pltpu.CompilerParams(vmem_limit_bytes=VMEM_LIMIT - 4 * before.size),
         name="last_stacks",
@@ -487,7 +502,7 @@
     picked = pick_sources(record[0], valid, sources)
     before, receiver, source = gather_stacks(record[0], valid, picked, wide_count, rep_count)
     scale = 1.0 / math.sqrt(wide_count * rep_count * (length // 2)) / RAISE
-    before = pltpu.with_memory_space_constraint(before, pltpu.VMEM)
+    before, receiver, source = (pltpu.with_memory_space_constraint(kept, pltpu.VMEM) for kept in (before, receiver, source))
     return last_stacks(source, receiver, before, scale, rep_count)
 
 

time: 305 us -> 302 us (level)
  no operation moved by 1% of the time
where the time goes in v3:
time: 302 us
  Pallas kernels  302 us (100%)
    pallas_call x1, Pallas kernels, gather_stacks(): pl.pallas_call(functools.partial(gather_kernel, wide_count, rep_count), i...  287 us
    pallas_call x1, Pallas kernels, last_stacks(): pl.pallas_call(functools.partial(last_kernel, scale), in_specs=[in_vmem]...  11.2 us

profile of v3, /device:TPU:0, one launch (start us, length us, event | category | flops | bytes accessed | tf_op | source)
XLA Modules:
  0.0 301.6 jit_solution(13637646541726200243)
XLA Ops:
  0.0 3.1 %pick_sources.1.picked_ref = bf16[192,256]{1,0:T(8,128)(2,1)} custom-call(s32[3]{0:T(128)} %blocks_ref.1, bf16[256,8192]{1,0:T(8,128)(2,1)} %bitcast.1, bf16[256,8192]{1,0:T(8,128)(2,1)} %bitcast.2, bf16[256,8192]{1,0:T(8,128)(2,1)} %bitcast.3, s32[1,8192]{1,0:T(1,128)} %valid_ref.1, s32[1,8192]{1,0:T(1,128)} %valid_ref.1, s32[1,8192]{1,0:T(1,128)} %valid_ref.1, ...), custom_call_target="tpu_custom_call" | custom-call | tf_op jit(solution)/shard_map/pick_sources/pallas_call | solution.py:110
  3.1 287.2 %gather_stacks.1 = (f32[6144,1024]{1,0:T(8,128)S(1)}, bf16[256,1024]{1,0:T(8,128)(2,1)S(1)}, bf16[192,256]{1,0:T(8,128)(2,1)S(1)}) custom-call(bf16[256,8192]{1,0:T(8,128)(2,1)} %bitcast.4, s32[1,8192]{1,0:T(1,128)} %valid_ref.1, bf16[192,256]{1,0:T(8,128)(2,1)} %pick_sources.1.picked_ref, bf16[256,256]{1,0:T(8,128)(2,1)} %constant.12.clone.refs_6_.table_ref, ...), custom_call_target="tpu_custom_call" | custom-call | flops 206158430208 | bytes 25165824 | tf_op jit(solution)/shard_map/gather_stacks/pallas_call | solution.py:394
  290.4 11.2 %last_stacks.1 = f32[32,192,1024]{2,1,0:T(8,128)} custom-call(bf16[192,256]{1,0:T(8,128)(2,1)S(1)} %get-tuple-element.8.source_ref, f32[128,2,128]{2,1,0:T(2,128)} %constant.14.clone.rotation_ref, bf16[256,1024]{1,0:T(8,128)(2,1)S(1)} %get-tuple-element.9.receiver_ref, f32[6144,1024]{1,0:T(8,128)S(1)} %get-tuple-element.10.before_ref), custom_call_target="tpu_custom_call" | custom-call | tf_op jit(solution)/shard_map/last_stacks/pallas_call | solution.py:480

commit v4 on v3

--- a/solution.py
+++ b/solution.py
@@ -17,6 +17,7 @@
 
 VMEM_LIMIT = 56 * 1024 * 1024
 TILE_LAGS = 4
+LAST_TILE_LAGS = 8
 PAIR = 2
 RAISE = 2.0**16
 MESH = pl.DeviceIdType.MESH
@@ -476,7 +477,7 @@
     rows, length = source.shape
     channels = receiver.shape[1]
     in_vmem = pl.BlockSpec(memory_space=pltpu.VMEM)
-    half = [pltpu.VMEM((TILE_LAGS * rows, length), jnp.bfloat16), pltpu.VMEM((TILE_LAGS * rows, length), jnp.float8_e5m2)]
+    half = [pltpu.VMEM((LAST_TILE_LAGS * rows, length), jnp.bfloat16), pltpu.VMEM((LAST_TILE_LAGS * rows, length), jnp.float8_e5m2)]
     return pl.pallas_call(
         functools.partial(last_kernel, scale),
         in_specs=[in_vmem] * 4,
@@ -486,8 +487,8 @@
             *half,
             *half,
             pltpu.VMEM((length, channels), jnp.float8_e5m2),
-            pltpu.VMEM((TILE_LAGS, rows, channels), jnp.float32),
-            pltpu.VMEM((TILE_LAGS, rows, channels), jnp.float32),
+            pltpu.VMEM((LAST_TILE_LAGS, rows, channels), jnp.float32),
+            pltpu.VMEM((LAST_TILE_LAGS, rows, channels), jnp.float32),
             pltpu.SemaphoreType.DMA((2, channels // min(256, channels))),
         ],
         compiler_params=pltpu.CompilerParams(vmem_limit_bytes=VMEM_LIMIT - 4 * before.size),

time: 302 us -> 302 us (level)
  no operation moved by 1% of the time
where the time goes in v4:
time: 302 us
  Pallas kernels  302 us (100%)
    pallas_call x1, Pallas kernels, gather_stacks(): pl.pallas_call(functools.partial(gather_kernel, wide_count, rep_count), i...  287 us
    pallas_call x1, Pallas kernels, last_stacks(): pl.pallas_call(functools.partial(last_kernel, scale), in_specs=[in_vmem]...  11.4 us

profile of v4, /device:TPU:0, one launch (start us, length us, event | category | flops | bytes accessed | tf_op | source)
XLA Modules:
  0.0 302.0 jit_solution(5484477710324916300)
XLA Ops:
  0.0 3.1 %pick_sources.1.picked_ref = bf16[192,256]{1,0:T(8,128)(2,1)} custom-call(s32[3]{0:T(128)} %blocks_ref.1, bf16[256,8192]{1,0:T(8,128)(2,1)} %bitcast.1, bf16[256,8192]{1,0:T(8,128)(2,1)} %bitcast.2, bf16[256,8192]{1,0:T(8,128)(2,1)} %bitcast.3, s32[1,8192]{1,0:T(1,128)} %valid_ref.1, s32[1,8192]{1,0:T(1,128)} %valid_ref.1, s32[1,8192]{1,0:T(1,128)} %valid_ref.1, ...), custom_call_target="tpu_custom_call" | custom-call | tf_op jit(solution)/shard_map/pick_sources/pallas_call | solution.py:111
  3.1 287.2 %gather_stacks.1 = (f32[6144,1024]{1,0:T(8,128)S(1)}, bf16[256,1024]{1,0:T(8,128)(2,1)S(1)}, bf16[192,256]{1,0:T(8,128)(2,1)S(1)}) custom-call(bf16[256,8192]{1,0:T(8,128)(2,1)} %bitcast.4, s32[1,8192]{1,0:T(1,128)} %valid_ref.1, bf16[192,256]{1,0:T(8,128)(2,1)} %pick_sources.1.picked_ref, bf16[256,256]{1,0:T(8,128)(2,1)} %constant.12.clone.refs_6_.table_ref, ...), custom_call_target="tpu_custom_call" | custom-call | flops 206158430208 | bytes 25165824 | tf_op jit(solution)/shard_map/gather_stacks/pallas_call | solution.py:395
  290.4 11.4 %last_stacks.1 = f32[32,192,1024]{2,1,0:T(8,128)} custom-call(bf16[192,256]{1,0:T(8,128)(2,1)S(1)} %get-tuple-element.8.source_ref, f32[128,2,128]{2,1,0:T(2,128)} %constant.14.clone.rotation_ref, bf16[256,1024]{1,0:T(8,128)(2,1)S(1)} %get-tuple-element.9.receiver_ref, f32[6144,1024]{1,0:T(8,128)S(1)} %get-tuple-element.10.before_ref), custom_call_target="tpu_custom_call" | custom-call | tf_op jit(solution)/shard_map/last_stacks/pallas_call | solution.py:481
